TPU v7x, 256 devices: a whole 4x4x8 slice. The times are simulated.
256 devices in a mesh: prow: 8 (over x, y_lo), pcol: 32 (over y_hi, z, core).
Axes of the slice: x: 4, y: 4 (y_hi: 2, y_lo: 2; y = y_hi * 2 + y_lo), z: 8, core: 2. Of those that a mesh axis runs over, the one named last changes fastest.
Arguments:
- anc_inverse: bfloat16 [12, 2048, 3, 8192], P(None, 'prow', None, 'pcol'), may hold values from -0.0390625 to 0.0390625
- panel: bfloat16 [3, 12, 8, 256, 512], P(None, None, 'prow', 'pcol'), may hold values from -1.1953125 to 1.1953125
- tile_mask: int32 [3, 96], replicated, may hold values 0 or 1
- diag_inverse: float32 [3, 512, 512], P(None, ('prow', 'pcol')), may hold values from -6 to 6
Outputs:
- block_column: bfloat16 [3, 12, 8, 256, 512], P(None, None, 'prow', 'pcol')
- diag_block: float32 [3, 512, 512], P(None, ('prow', 'pcol'))
All inputs are finite; a program needn't handle non-finite values.
Results may differ from a plain program's by a relative error of at most 0.0017.
Values may be sent and summed in bfloat16 or wider, within the bound.
A program may use at most 128 MiB of HBM per device.

v0:
```python
import jax
import jax.numpy as jnp
from jax import lax
from jax.sharding import PartitionSpec as P


def spread(x, axis, root):
    mine = lax.axis_index(axis) == root
    return lax.psum(jnp.where(mine, x, jnp.zeros_like(x)), axis)


def local_product(anc_block, columns):
    return jnp.einsum("aibj,sbjw->isaw", anc_block, columns, preferred_element_type=jnp.float32)


def outbound(masked, n_row, n_col):
    groups, tile_rows, single, sub_rows, width = masked.shape
    tile_cols = tile_rows * n_row // n_col
    grouped = masked.reshape(groups, tile_cols, n_col // n_row, sub_rows, width)
    return jnp.repeat(grouped, n_row, axis=2)


def body(anc_inverse, panel, tile_mask, diag_inverse):
    n_row = lax.axis_size("prow")
    n_col = lax.axis_size("pcol")
    row_pos = lax.axis_index("prow")
    col_pos = lax.axis_index("pcol")
    sets, tile_rows, single, sub_rows, width = panel.shape
    tiles = tile_mask.shape[1]
    tile_size = anc_inverse.shape[1]
    row_ids = jnp.arange(tile_rows, dtype=jnp.int32) * n_row + row_pos
    hits = (row_ids[:, None] == jnp.arange(tiles, dtype=jnp.int32)[None, :]).astype(jnp.int32)
    row_mask = jnp.sum(tile_mask[:, None, :] * hits[None], axis=2)
    keep = row_mask.astype(jnp.bfloat16)[:, :, None, None, None]
    masked = panel * keep
    outgoing = outbound(masked, n_row, n_col)
    root = col_pos % n_row
    pieces = []
    for index in range(sets):
        arrived = lax.all_to_all(
            outgoing[index : index + 1], "pcol", split_axis=2, concat_axis=3, tiled=True
        )
        columns = spread(arrived.reshape(1, -1, tile_size, width), "prow", root)
        pieces.append(
            lax.psum_scatter(
                local_product(anc_inverse, columns), "pcol", scatter_dimension=0, tiled=True
            )
        )
    summed = jnp.concatenate(pieces, axis=1)
    image = -jnp.transpose(summed, (1, 2, 0, 3))[:, :, None] * keep.astype(jnp.float32)
    block_column = image.astype(jnp.bfloat16)
    partial_value = jnp.einsum(
        "saxiw,saxiv->swv", masked, block_column, preferred_element_type=jnp.float32
    )
    mine = lax.psum_scatter(partial_value, ("prow", "pcol"), scatter_dimension=1, tiled=True)
    diag_block = diag_inverse - mine
    return (block_column, diag_block)


def solution(mesh):
    in_specs = (
        P(None, "prow", None, "pcol"),
        P(None, None, "prow", "pcol", None),
        P(),
        P(None, ("prow", "pcol"), None),
    )
    out_specs = (P(None, None, "prow", "pcol", None), P(None, ("prow", "pcol"), None))
    return jax.shard_map(body, mesh=mesh, in_specs=in_specs, out_specs=out_specs, check_vma=False)
```

profile of v0, /device:TPU:2, one launch (start us, length us, event | category | flops | bytes accessed | tf_op | source)
XLA Modules:
  0.0 1114.2 jit_solution(5080620004551118241)
XLA Ops:
  7.2 0.1 fusion.10
  7.3 0.8 multiply_reduce_fusion
  8.1 1.1 broadcast_multiply_fusion
  9.2 1.0 broadcast_in_dim.23
  10.2 11.5 %all-to-all-start.2 = ((bf16[1,3,32,8,512]{4,3,1,0,2:T(8,128)(2,1)}), bf16[1,3,32,8,512]{4,3,1,0,2:T(8,128)(2,1)S(1)}, u32[]{:S(2)}, u32[]{:S(2)}) async-start(bf16[1,3,32,8,512]{4,3,1,0,2:T(8,128)(2,1)} %bitcast.17), calls=%async_computation.2 | async-start | bytes 1572864 | tf_op jit(solution)/shard_map/all_to_all | solution.py:40
  21.7 24.8 %all-to-all-done.2 = bf16[1,3,32,8,512]{4,3,1,0,2:T(8,128)(2,1)S(1)} async-done(((bf16[1,3,32,8,512]{4,3,1,0,2:T(8,128)(2,1)}), bf16[1,3,32,8,512]{4,3,1,0,2:T(8,128)(2,1)S(1)}, u32[]{:S(2)}, u32[]{:S(2)}) %all-to-all-start.2) | async-done | bytes 786464 | tf_op jit(solution)/shard_map/all_to_all | solution.py:40
  46.5 1.0 broadcast_in_dim.21
  47.5 3.9 all-to-all-start.1
  51.4 24.8 %all-to-all-done.1 = bf16[1,3,32,8,512]{4,3,1,0,2:T(8,128)(2,1)S(1)} async-done(((bf16[1,3,32,8,512]{4,3,1,0,2:T(8,128)(2,1)}), bf16[1,3,32,8,512]{4,3,1,0,2:T(8,128)(2,1)S(1)}, u32[]{:S(2)}, u32[]{:S(2)}) %all-to-all-start.1) | async-done | bytes 786464 | tf_op jit(solution)/shard_map/all_to_all | solution.py:40
  76.2 1.0 broadcast_in_dim.19
  77.2 3.9 all-to-all-start
  81.1 0.0 all-reduce.17.cloned.1.call-start
  81.1 0.1 fusion.3
  81.2 1.2 copy.44
  82.4 0.1 fusion.4
  82.5 1.2 copy.40
  83.6 22.3 %all-to-all-done = bf16[1,3,32,8,512]{4,3,1,0,2:T(8,128)(2,1)S(1)} async-done(((bf16[1,3,32,8,512]{4,3,1,0,2:T(8,128)(2,1)}), bf16[1,3,32,8,512]{4,3,1,0,2:T(8,128)(2,1)S(1)}, u32[]{:S(2)}, u32[]{:S(2)}) %all-to-all-start) | async-done | bytes 786464 | tf_op jit(solution)/shard_map/all_to_all | solution.py:40
  105.9 0.1 fusion.5
  106.0 1.2 copy.36
  107.1 0.0 all-reduce.17.cloned.1.call-update
  107.1 0.0 all-reduce.11.cloned.1.call-start
  107.2 114.8 %all-reduce.17.cloned.1.call-done = (bf16[3,256,512]{1,2,0:T(8,128)(2,1)}, bf16[3,256,512]{1,2,0:T(8,128)(2,1)}, bf16[3,256,512]{1,2,0:T(8,128)(2,1)}) async-done(((bf16[3,256,512]{1,2,0:T(8,128)(2,1)}, bf16[3,256,512]{1,2,0:T(8,128)(2,1)}, bf16[3,256,512]{1,2,0:T(8,128)(2,1)}), (bf16[3,256,512]{1,2,0:T(8,128)(2,1)}, bf16[3,256,512]{1,2,0:T(8,128)(2,1)}, ...) | async-done | bytes 2359312 | tf_op jit(solution)/shard_map/psum | solution.py:9
  222.0 7.9 convolution_bitcast_fusion.2
  229.9 16.0 %copy.37 = f32[256,1,12,512]{3,1,2,0:T(1,128)} copy(f32[256,1,12,512]{0,3,2,1:T(8,128)} %convolution_bitcast_fusion.2) | data formatting | bytes 12582912 | tf_op jit(solution)/shard_map/aibj,sbjw->isaw/transpose | solution.py:13
  245.9 0.0 all-reduce.11.cloned.1.call-update
  245.9 0.0 all-reduce.15.cloned.1.call-start
  246.0 1.1 copy-done.2
  247.0 6.9 convolution_bitcast_fusion
  253.9 16.0 %copy.45 = f32[256,1,12,512]{3,1,2,0:T(1,128)} copy(f32[256,1,12,512]{0,3,2,1:T(8,128)} %convolution_bitcast_fusion) | data formatting | bytes 12582912 | tf_op jit(solution)/shard_map/aibj,sbjw->isaw/transpose | solution.py:13
  269.9 6.9 convolution_bitcast_fusion.1
  276.8 16.1 %copy.41 = f32[256,1,12,512]{3,1,2,0:T(1,128)} copy(f32[256,1,12,512]{0,3,2,1:T(8,128)} %convolution_bitcast_fusion.1) | data formatting | bytes 12582912 | tf_op jit(solution)/shard_map/aibj,sbjw->isaw/transpose | solution.py:13
  292.9 0.0 all-reduce.15.cloned.1.call-update
  292.9 0.0 all-reduce.13.cloned.1.call-start
  293.0 0.6 copy-done.3
  293.6 0.6 dynamic-slice
  294.8 237.6 %all-reduce.11.cloned.1.call-done = f32[256,1,12,512]{3,1,2,0:T(1,128)} async-done(((f32[256,1,12,512]{3,1,2,0:T(1,128)}), f32[256,1,12,512]{3,1,2,0:T(1,128)}) %all-reduce.11.cloned.1.call-update) | async-done | bytes 6291472
  532.4 0.9 constant_dynamic-slice_fusion.2
  533.3 0.1 copy.46
  533.4 304.8 %all-reduce.15.cloned.1.call-done = (f32[256,1,12,512]{3,1,2,0:T(1,128)}, f32[256,1,12,512]{3,1,2,0:T(1,128)}) async-done(((f32[256,1,12,512]{3,1,2,0:T(1,128)}, f32[256,1,12,512]{3,1,2,0:T(1,128)}), (f32[256,1,12,512]{3,1,2,0:T(1,128)}, f32[256,1,12,512]{3,1,2,0:T(1,128)})) %all-reduce.15.cloned.1.call-update) | async-done | bytes 12582928
  838.2 1.3 constant_dynamic-slice_fusion
  839.5 0.1 copy.48
  839.5 0.1 copy.47
  839.6 0.0 copy-start
  839.6 2.3 convolution_bitcast_fusion.3
  841.9 0.0 all-reduce.13.cloned.1.call-update
  842.0 0.8 fusion.11
  842.8 263.5 %all-reduce.13.cloned.1.call-done = f32[3,512,512]{2,1,0:T(8,128)} async-done(((f32[3,512,512]{2,1,0:T(8,128)}), f32[3,512,512]{2,1,0:T(8,128)}) %all-reduce.13.cloned.1.call-update) | async-done | bytes 3145744
  1106.3 1.4 dynamic-slice_subtract_fusion
  (11 shorter events, 0.1 us)
Async XLA Ops:
  10.2 36.3 %all-to-all-start.2 = ((bf16[1,3,32,8,512]{4,3,1,0,2:T(8,128)(2,1)}), bf16[1,3,32,8,512]{4,3,1,0,2:T(8,128)(2,1)S(1)}, u32[]{:S(2)}, u32[]{:S(2)}) async-start(bf16[1,3,32,8,512]{4,3,1,0,2:T(8,128)(2,1)} %bitcast.17), calls=%async_computation.2 | async-start | bytes 1572864 | tf_op jit(solution)/shard_map/all_to_all | solution.py:40
  47.5 28.7 %all-to-all-start.1 = ((bf16[1,3,32,8,512]{4,3,1,0,2:T(8,128)(2,1)}), bf16[1,3,32,8,512]{4,3,1,0,2:T(8,128)(2,1)S(1)}, u32[]{:S(2)}, u32[]{:S(2)}) async-start(bf16[1,3,32,8,512]{4,3,1,0,2:T(8,128)(2,1)} %bitcast.9), calls=%async_computation.1 | async-start | bytes 1572864 | tf_op jit(solution)/shard_map/all_to_all | solution.py:40
  77.2 28.7 %all-to-all-start = ((bf16[1,3,32,8,512]{4,3,1,0,2:T(8,128)(2,1)}), bf16[1,3,32,8,512]{4,3,1,0,2:T(8,128)(2,1)S(1)}, u32[]{:S(2)}, u32[]{:S(2)}) async-start(bf16[1,3,32,8,512]{4,3,1,0,2:T(8,128)(2,1)} %bitcast.1), calls=%async_computation | async-start | bytes 1572864 | tf_op jit(solution)/shard_map/all_to_all | solution.py:40
  81.1 140.9 %all-reduce.17.cloned.1.call-start = ((), (), s32[]{:S(2)}) async-start(), calls=%async_computation.6 | async-start | bytes 4718592 | tf_op jit(solution)/shard_map/psum | solution.py:9
  107.1 425.2 %all-reduce.11.cloned.1.call-start = ((), (), s32[]{:S(2)}) async-start(), calls=%async_computation.3 | async-start | bytes 12582912
  245.9 1.1 copy-start.2
  245.9 592.3 %all-reduce.15.cloned.1.call-start = ((), (), s32[]{:S(2)}) async-start(), calls=%async_computation.5 | async-start | bytes 25165824
  253.9 16.0 %copy-start.1 = (bf16[3,256,512]{1,2,0:T(8,128)(2,1)S(1)}, bf16[3,256,512]{1,2,0:T(8,128)(2,1)}, u32[]{:S(2)}) copy-start(bf16[3,256,512]{1,2,0:T(8,128)(2,1)} %get-tuple-element.13) | copy-start | bytes 2359300
  292.9 0.7 copy-start.3
  292.9 813.4 %all-reduce.13.cloned.1.call-start = ((), (), s32[]{:S(2)}) async-start(), calls=%async_computation.4 | async-start | bytes 6291456
  839.6 266.7 %copy-start = (f32[3,2,512]{2,1,0:T(2,128)S(1)}, f32[3,2,512]{2,1,0:T(2,128)}, u32[]{:S(2)}) copy-start(f32[3,2,512]{2,1,0:T(2,128)} %param.7) | copy-start | bytes 36868
Sparse Core Ops, SparseCore 0:
  107.3 114.6 all-reduce.16
  246.0 286.2 all-reduce.10
  535.1 303.0 all-reduce.14
  843.4 262.7 all-reduce.12
where the time goes:
time: 1120 us; the launch traced here: 1110 us
  waiting for transfers between devices  993 us (89%)
  local copies, waits for them, and re-layouts  59.3 us (5%)
  matrix products  23.9 us (2%)
  starting transfers between devices  19.5 us (2%)
  between operations  14.6 us (1%)
    unnamed x7, waiting for transfers between devices  806 us
    psum x1, waiting for transfers between devices, spread(): return lax.psum(jnp.where(mine, x, jnp.zeros_like(x)), axis)  115 us
    all_to_all x3, waiting for transfers between devices, body(): lax.all_to_all(outgoing[index:index + 1], 'pcol', split_axis=2, concat_ax...  71.9 us
    transpose x3, local copies, waits for them, and re-layouts, local_product(): jnp.einsum('aibj,sbjw->isaw', anc_block, columns, preferred_element_type=...  48.2 us
  transfers between devices with their start and end apart: 7, of which 7 were waited for; matrix products, arithmetic and copies ran while one was open for 5% of the time, Pallas kernels for 0%

commit v1 on v0

--- a/solution.py
+++ b/solution.py
@@ -6,7 +6,7 @@
 
 def spread(x, axis, root):
     mine = lax.axis_index(axis) == root
-    return lax.psum(jnp.where(mine, x, jnp.zeros_like(x)), axis)
+    return jnp.sum(lax.all_gather(jnp.where(mine, x, jnp.zeros_like(x)), axis), axis=0)
 
 
 def local_product(anc_block, columns):

time: 1120 us -> 1330 us (1.19)
  waiting for transfers between devices: 993 us -> 1150 us
  blocking collectives: 0 us -> 56.5 us
  other arithmetic: 4.39 us -> 18.7 us
    all_gather x0 -> x3, waiting for transfers between devices: none -> 299 us  [spread(): lax.all_gather(jnp.where(mine, x, jnp.zeros_like(x)), axis)]
    psum x1 -> x0, waiting for transfers between devices: 115 us -> none  [spread(): return lax.psum(jnp.where(mine, x, jnp.zeros_like(x)), axis)]
    all_to_all x0 -> x2, blocking collectives: none -> 56.5 us  [body(): lax.all_to_all(outgoing[index:index + 1], 'pcol', split_axis=2, concat_ax...]
    all_to_all x3 -> x1, waiting for transfers between devices: 71.9 us -> 24.8 us  [body(): lax.all_to_all(outgoing[index:index + 1], 'pcol', split_axis=2, concat_ax...]
    unnamed x7 -> x9, waiting for transfers between devices: 806 us -> 827 us
  transfers between devices with their start and end apart: 7 -> 7, of which waited for: 7 -> 7; matrix products, arithmetic and copies ran while one was open for 5% -> 6% of each run, Pallas kernels for 0% -> 0%
where the time goes in v1:
time: 1330 us
  waiting for transfers between devices  1150 us (86%)
  blocking collectives  56.5 us (4%)
  local copies, waits for them, and re-layouts  52.9 us (4%)
  matrix products  23.1 us (2%)
  other arithmetic  18.7 us (1%)
  between operations  14.9 us (1%)
    unnamed x9, waiting for transfers between devices  827 us
    all_gather x3, waiting for transfers between devices, spread(): lax.all_gather(jnp.where(mine, x, jnp.zeros_like(x)), axis)  299 us
    all_to_all x2, blocking collectives, body(): lax.all_to_all(outgoing[index:index + 1], 'pcol', split_axis=2, concat_ax...  56.5 us
    transpose x3, local copies, waits for them, and re-layouts, local_product(): jnp.einsum('aibj,sbjw->isaw', anc_block, columns, preferred_element_type=...  48.2 us
  transfers between devices with their start and end apart: 7, of which 7 were waited for; matrix products, arithmetic and copies ran while one was open for 6% of the time, Pallas kernels for 0%

profile of v1, /device:TPU:2, one launch (start us, length us, event | category | flops | bytes accessed | tf_op | source)
XLA Modules:
  0.0 1328.6 jit_solution(6946905725899806248)
XLA Ops:
  7.2 0.1 fusion.10
  7.3 0.8 multiply_reduce_fusion
  8.1 1.1 broadcast_multiply_fusion
  9.2 1.0 broadcast_in_dim.19
  10.2 11.5 all-to-all-start
  21.7 0.0 all-gather.4.cloned.1.call-start
  21.7 24.8 %all-to-all-done = bf16[1,3,32,8,512]{4,3,1,0,2:T(8,128)(2,1)S(1)} async-done(((bf16[1,3,32,8,512]{4,3,1,0,2:T(8,128)(2,1)}), bf16[1,3,32,8,512]{4,3,1,0,2:T(8,128)(2,1)S(1)}, u32[]{:S(2)}, u32[]{:S(2)}) %all-to-all-start) | async-done | bytes 786464 | tf_op jit(solution)/shard_map/all_to_all | solution.py:40
  46.5 0.9 fusion.5
  47.4 0.0 all-gather.4.cloned.1.call-update
  47.4 0.0 all-gather.8.cloned.1.call-start
  47.5 0.1 broadcast_in_dim.23
  47.6 28.1 %all_to_all.12 = bf16[1,3,32,8,512]{4,3,1,0,2:T(8,128)(2,1)S(1)} all-to-all(bf16[1,3,32,8,512]{4,3,1,0,2:T(8,128)(2,1)S(1)} %bitcast.59), channel_id=1, replica_groups=mesh['prow'=8,'pcol'=32] {'pcol'}, dimensions={2} | all-to-all | bytes 1572864 | tf_op jit(solution)/shard_map/all_to_all | solution.py:40
  75.7 1.0 fusion.3
  76.7 0.0 all-gather.8.cloned.1.call-update
  76.7 0.0 all-gather.6.cloned.1.call-start
  76.8 0.1 broadcast_in_dim.21
  76.8 28.4 %all_to_all.13 = bf16[1,3,32,8,512]{4,3,1,0,2:T(8,128)(2,1)S(1)} all-to-all(bf16[1,3,32,8,512]{4,3,1,0,2:T(8,128)(2,1)S(1)} %bitcast.60), channel_id=1, replica_groups=mesh['prow'=8,'pcol'=32] {'pcol'}, dimensions={2} | all-to-all | bytes 1572864 | tf_op jit(solution)/shard_map/all_to_all | solution.py:40
  105.2 0.9 fusion.4
  106.2 0.0 all-gather.6.cloned.1.call-update
  106.2 0.0 all-reduce.9.cloned.1.call-start
  106.3 83.4 %all-gather.4.cloned.1.call-done = bf16[8,1,3,256,512]{4,3,2,1,0:T(8,128)(2,1)} async-done(((bf16[1,1,3,256,512]{4,3,2,1,0:T(8,128)(2,1)}), bf16[8,1,3,256,512]{4,3,2,1,0:T(8,128)(2,1)}) %all-gather.4.cloned.1.call-update) | async-done | bytes 6291472 | tf_op jit(solution)/shard_map/all_gather | solution.py:9
  189.7 3.9 reduce_sum.46
  193.5 6.9 convolution_bitcast_fusion.2
  200.5 16.0 %copy.53 = f32[256,1,12,512]{3,1,2,0:T(1,128)} copy(f32[256,1,12,512]{0,3,2,1:T(8,128)} %convolution_bitcast_fusion.2) | data formatting | bytes 12582912 | tf_op jit(solution)/shard_map/aibj,sbjw->isaw/transpose | solution.py:13
  216.5 0.0 all-reduce.9.cloned.1.call-update
  216.5 0.0 all-reduce.13.cloned.1.call-start
  216.6 107.4 %all-gather.8.cloned.1.call-done = bf16[8,1,3,256,512]{4,3,2,1,0:T(8,128)(2,1)} async-done(((bf16[1,1,3,256,512]{4,3,2,1,0:T(8,128)(2,1)}), bf16[8,1,3,256,512]{4,3,2,1,0:T(8,128)(2,1)}) %all-gather.8.cloned.1.call-update) | async-done | bytes 6291472 | tf_op jit(solution)/shard_map/all_gather | solution.py:9
  324.0 3.9 reduce_sum.48
  327.8 6.9 convolution_bitcast_fusion
  334.8 16.0 %copy.61 = f32[256,1,12,512]{3,1,2,0:T(1,128)} copy(f32[256,1,12,512]{0,3,2,1:T(8,128)} %convolution_bitcast_fusion) | data formatting | bytes 12582912 | tf_op jit(solution)/shard_map/aibj,sbjw->isaw/transpose | solution.py:13
  350.8 108.1 %all-gather.6.cloned.1.call-done = bf16[8,1,3,256,512]{4,3,2,1,0:T(8,128)(2,1)} async-done(((bf16[1,1,3,256,512]{4,3,2,1,0:T(8,128)(2,1)}), bf16[8,1,3,256,512]{4,3,2,1,0:T(8,128)(2,1)}) %all-gather.6.cloned.1.call-update) | async-done | bytes 6291472 | tf_op jit(solution)/shard_map/all_gather | solution.py:9
  458.9 3.9 reduce_sum.47
  462.7 6.9 convolution_bitcast_fusion.1
  469.7 16.1 %copy.57 = f32[256,1,12,512]{3,1,2,0:T(1,128)} copy(f32[256,1,12,512]{0,3,2,1:T(8,128)} %convolution_bitcast_fusion.1) | data formatting | bytes 12582912 | tf_op jit(solution)/shard_map/aibj,sbjw->isaw/transpose | solution.py:13
  485.8 0.0 all-reduce.11.cloned.1.call-start
  485.8 0.6 copy-done.1
  486.4 0.6 dynamic-slice
  487.7 258.9 %all-reduce.9.cloned.1.call-done = f32[256,1,12,512]{3,1,2,0:T(1,128)} async-done(((f32[256,1,12,512]{3,1,2,0:T(1,128)}), f32[256,1,12,512]{3,1,2,0:T(1,128)}) %all-reduce.9.cloned.1.call-update) | async-done | bytes 6291472
  746.5 0.9 constant_dynamic-slice_fusion.2
  747.5 0.1 copy.62
  747.6 304.6 %all-reduce.13.cloned.1.call-done = (f32[256,1,12,512]{3,1,2,0:T(1,128)}, f32[256,1,12,512]{3,1,2,0:T(1,128)}) async-done(((f32[256,1,12,512]{3,1,2,0:T(1,128)}, f32[256,1,12,512]{3,1,2,0:T(1,128)}), (f32[256,1,12,512]{3,1,2,0:T(1,128)}, f32[256,1,12,512]{3,1,2,0:T(1,128)})) %all-reduce.13.cloned.1.call-update) | async-done | bytes 12582928
  1052.2 1.3 constant_dynamic-slice_fusion
  1053.5 0.1 copy.64
  1053.6 0.1 copy.63
  1053.7 2.3 convolution_bitcast_fusion.3
  1056.0 0.8 fusion.11
  1056.8 263.5 %all-reduce.11.cloned.1.call-done = f32[3,512,512]{2,1,0:T(8,128)} async-done(((f32[3,512,512]{2,1,0:T(8,128)}), f32[3,512,512]{2,1,0:T(8,128)}) %all-reduce.11.cloned.1.call-update) | async-done | bytes 3145744
  1320.3 1.4 dynamic-slice_subtract_fusion
  (11 shorter events, 0.1 us)
Async XLA Ops:
  10.2 36.3 %all-to-all-start = ((bf16[1,3,32,8,512]{4,3,1,0,2:T(8,128)(2,1)}), bf16[1,3,32,8,512]{4,3,1,0,2:T(8,128)(2,1)S(1)}, u32[]{:S(2)}, u32[]{:S(2)}) async-start(bf16[1,3,32,8,512]{4,3,1,0,2:T(8,128)(2,1)} %bitcast.1), calls=%async_computation | async-start | bytes 1572864 | tf_op jit(solution)/shard_map/all_to_all | solution.py:40
  21.7 168.0 %all-gather.4.cloned.1.call-start = ((), (), s32[]{:S(2)}) async-start(), calls=%async_computation.3 | async-start | bytes 7077888 | tf_op jit(solution)/shard_map/all_gather | solution.py:9
  47.4 276.5 %all-gather.8.cloned.1.call-start = ((), (), s32[]{:S(2)}) async-start(), calls=%async_computation.5 | async-start | bytes 7077888 | tf_op jit(solution)/shard_map/all_gather | solution.py:9
  76.7 382.1 %all-gather.6.cloned.1.call-start = ((), (), s32[]{:S(2)}) async-start(), calls=%async_computation.4 | async-start | bytes 7077888 | tf_op jit(solution)/shard_map/all_gather | solution.py:9
  106.2 640.3 %all-reduce.9.cloned.1.call-start = ((), (), s32[]{:S(2)}) async-start(), calls=%async_computation.6 | async-start | bytes 12582912
  216.5 835.7 %all-reduce.13.cloned.1.call-start = ((), (), s32[]{:S(2)}) async-start(), calls=%async_computation.8 | async-start | bytes 25165824
  485.7 0.7 copy-start.1
  485.8 834.6 %all-reduce.11.cloned.1.call-start = ((), (), s32[]{:S(2)}) async-start(), calls=%async_computation.7 | async-start | bytes 6291456
  1053.6 266.7 %copy-start = (f32[3,2,512]{2,1,0:T(2,128)S(1)}, f32[3,2,512]{2,1,0:T(2,128)}, u32[]{:S(2)}) copy-start(f32[3,2,512]{2,1,0:T(2,128)} %param.7) | copy-start | bytes 36868
Sparse Core Ops, SparseCore 0:
  47.6 142.0 all-gather.3
  191.5 132.4 all-gather.7
  325.8 133.0 all-gather.5
  461.4 285.1 all-reduce.8
  749.1 303.0 all-reduce.12
  1057.5 262.7 all-reduce.10
